TPU v7x, 32 devices: a whole 2x2x4 slice. The times are simulated.
32 devices in a mesh: gx: 4 (over y, x), gy: 4 (over z), gz: 2 (over core).
Axes of the slice: x: 2, y: 2, z: 4, core: 2. Of those that a mesh axis runs over, the one named last changes fastest.
Arguments:
- electroneg: float32 [4, 4, 2, 64, 128], P('gx', 'gy', 'gz'), may hold values from 1 to 9
- hardness: float32 [4, 4, 2, 64, 128], P('gx', 'gy', 'gz'), may hold values from 5 to 9
- tiles: float32 [4, 4, 2, 256, 128, 128], P('gx', 'gy', 'gz'), may hold values from -0.19 to 0.19
- pair_rows: int32 [4, 4, 2, 256], P('gx', 'gy', 'gz'), may hold values from 0 to 63
- pair_cols: int32 [4, 4, 2, 256], P('gx', 'gy', 'gz'), may hold values from 0 to 159, as said below
- pair_count: int32 [4, 4, 2], P('gx', 'gy', 'gz'), may hold values from 64 to 256
- ghost_ids: int32 [4, 4, 2, 6, 16], P('gx', 'gy', 'gz'), may hold values from 0 to 63, as said below
Outputs:
- solutions: float32 [2, 4, 4, 2, 64, 128], P(None, 'gx', 'gy', 'gz')
- charges: float32 [4, 4, 2, 64, 128], P('gx', 'gy', 'gz')
Inputs may be any that keep to these rules, and one draw needn't show every extreme that they name: `pair_cols`: each slot is a local block (below 64) or a ghost slot. `ghost_ids`: the 16 blocks that a brick sends through one face are distinct.
All inputs are finite; a program needn't handle non-finite values.
Results may differ from a plain program's by a relative error of at most 0.0001.
Values sent between devices are 32-bit elements; how exact they have to be, the bound alone decides.
A program may use at most 64 MiB of HBM per device.

v0:
```python
import functools

import jax
import jax.numpy as jnp
from jax import lax
from jax.experimental import pallas as pl
from jax.experimental.pallas import tpu as pltpu
from jax.sharding import PartitionSpec as P

ITERS = 3
CHUNKS = 8
F32 = jnp.float32
BF16 = jnp.bfloat16


def split(values):
    high = values.astype(BF16)
    return high, (values - high.astype(F32)).astype(BF16)


def dot(first, second):
    return lax.dot_general(first, second, (((1,), (0,)), ((), ())), preferred_element_type=F32)


def dot_nt(first, second):
    return lax.dot_general(first, second, (((1,), (1,)), ((), ())), preferred_element_type=F32)


def times(hot, parts):
    return dot(hot, parts[0]) + dot(hot, parts[1])


def half_sums(row):
    atoms = row.shape[1] // 2
    sums = [jnp.sum(row[:, s * atoms : (s + 1) * atoms], axis=1, keepdims=True) for s in (0, 1)]
    return jnp.concatenate([jnp.broadcast_to(s, (1, atoms)) for s in sums], axis=1)


def column_sum(values):
    return jnp.sum(values, axis=0, keepdims=True)


def kernel(
    sizes, blocks, ghosts, pairs, atoms,
    count_ref, electroneg_ref, hardness_ref, rows_ref, cols_ref, ghost_ref, tiles_ref,
    solutions_ref, charges_ref,
    raw, tile_high, tile_low, vectors, products, halo_out, halo_in, back_out, back_in,
    part_a, part_b, sum_a, sum_b,
    load_sem, halo_send, halo_recv, back_send, back_recv, a_send, a_recv, b_send, b_recv,
):
    nx, ny, nz = sizes
    ix, iy, iz = lax.axis_index("gx"), lax.axis_index("gy"), lax.axis_index("gz")
    chunk_rows = pairs * atoms // CHUNKS
    loads = []
    for c in range(CHUNKS):
        here = pl.ds(c * chunk_rows, chunk_rows)
        load = pltpu.make_async_copy(tiles_ref.at[here], raw.at[here], load_sem.at[c])
        load.start()
        loads.append(load)

    plane = [
        (lax.rem(ix + ox, nx), iy, lax.rem(iz + oz, nz))
        for ox in range(nx) for oz in range(nz) if ox or oz
    ]
    line = [(ix, lax.rem(iy + oy, ny), iz) for oy in range(1, ny)]
    faces = []
    for axis in range(3):
        for step in (1, -1):
            there, behind = [ix, iy, iz], [ix, iy, iz]
            there[axis] = lax.rem(there[axis] + step + sizes[axis], sizes[axis])
            behind[axis] = lax.rem(behind[axis] - step + sizes[axis], sizes[axis])
            faces.append((tuple(there), tuple(behind)))

    barrier = pltpu.get_barrier_semaphore()
    for peer in plane + line:
        pl.semaphore_signal(barrier, inc=1, device_id=peer, device_id_type=pl.DeviceIdType.MESH)
    pl.semaphore_wait(barrier, len(plane) + len(line))

    def remote(src, dst, send, recv, peer):
        copy = pltpu.make_async_remote_copy(
            src_ref=src, dst_ref=dst, send_sem=send, recv_sem=recv,
            device_id=peer, device_id_type=pl.DeviceIdType.MESH,
        )
        copy.start()
        return copy

    def exchange(out, into, send, recv, it, which):
        copies = []
        for f in range(6):
            here = pl.ds(f * ghosts, ghosts)
            copies.append(remote(
                out.at[it, here], into.at[it, here], send.at[it, f], recv.at[it, f],
                faces[f][which],
            ))
        return copies

    def wait_all(copies):
        for copy in copies:
            copy.wait()

    def gathered_sum(part, arrived, send, recv, it, peers):
        return [
            remote(part.at[it], arrived.at[it, k], send.at[it, k], recv.at[it, k], peer)
            for k, peer in enumerate(peers)
        ]

    def reduce_all(rows, it):
        zeros = jnp.zeros((8 - len(rows), 2 * atoms), F32)
        part_a[it] = jnp.concatenate(rows + [zeros], axis=0)
        wait_all(gathered_sum(part_a, sum_a, a_send, a_recv, it, plane))
        total = part_a[it]
        for k in range(len(plane)):
            total = total + sum_a[it, k]
        part_b[it] = total
        wait_all(gathered_sum(part_b, sum_b, b_send, b_recv, it, line))
        for k in range(len(line)):
            total = total + sum_b[it, k]
        return [half_sums(total[i : i + 1]) for i in range(len(rows))]

    slots = 2 * atoms
    live = lax.broadcasted_iota(jnp.int32, (slots, pairs), 1) < count_ref[0, 0]
    slot_of = lax.broadcasted_iota(jnp.int32, (slots, pairs), 0)
    hot_rows = jnp.where((slot_of == rows_ref[...]) & live, 1.0, 0.0)
    hot_cols = jnp.where((slot_of == cols_ref[...]) & live, 1.0, 0.0)
    hot_ghost = jnp.where(
        lax.broadcasted_iota(jnp.int32, (atoms, atoms), 0) == ghost_ref[...], 1.0, 0.0
    )
    pick_rows = jnp.transpose(hot_rows)[:, :atoms].astype(BF16)
    pick_cols = jnp.transpose(hot_cols).astype(BF16)
    pick_ghost = jnp.transpose(hot_ghost).astype(BF16)
    hot_rows = hot_rows[:blocks].astype(BF16)
    hot_cols = hot_cols[: blocks + 6 * ghosts].astype(BF16)
    hot_ghost = hot_ghost[:blocks].astype(BF16)
    pad_rows = jnp.zeros((atoms - blocks, 2 * atoms), F32)
    pad_slots = jnp.zeros((slots - blocks - 6 * ghosts, 2 * atoms), F32)
    pad_ghost = jnp.zeros((atoms - 6 * ghosts, 2 * atoms), F32)

    row8 = lax.broadcasted_iota(jnp.int32, (8, atoms), 0)
    keep_high = jnp.where(row8 % 4 < 2, 1.0, 0.0)
    first_pair = row8 < 4

    def put_vectors(high, low):
        for k, part in enumerate((high, low)):
            vectors[pl.ds(2 * k, pairs, stride=4), :] = part[:, :atoms]
            vectors[pl.ds(2 * k + 1, pairs, stride=4), :] = part[:, atoms:]

    def take_products():
        first = [products[pl.ds(k, pairs, stride=4), :] for k in range(4)]
        return jnp.concatenate([first[0] + first[2], first[1] + first[3]], axis=1)

    def tile_loop(backward):
        def step(i, carry):
            at = pl.ds(pl.multiple_of(i * 8, 8), 8)
            here = pl.ds(pl.multiple_of(i * 2 * atoms, 2 * atoms), 2 * atoms)
            both = vectors[at, :]
            all_parts = both.astype(BF16)
            high_part = (both * keep_high).astype(BF16)
            high, low = tile_high[here, :], tile_low[here, :]
            if backward:
                lhs = jnp.concatenate([all_parts, high_part], axis=1)
                pair = [
                    jnp.concatenate([high[s * atoms : (s + 1) * atoms], low[s * atoms : (s + 1) * atoms]], axis=0)
                    for s in (0, 1)
                ]
                out = dot(lhs, jnp.concatenate(pair, axis=1))
            else:
                out = dot_nt(all_parts, high) + dot_nt(high_part, low)
            products[at, :] = jnp.where(first_pair, out[:, :atoms], out[:, atoms:])
            return carry

        lax.fori_loop(0, pairs // 2, step, 0, unroll=8)

    hardness = hardness_ref[...]
    hardness = jnp.concatenate([hardness, hardness], axis=1)
    electroneg = electroneg_ref[...]
    residual = jnp.concatenate([-electroneg, -jnp.ones_like(electroneg)], axis=1)
    direction = residual
    solutions = jnp.zeros_like(residual)

    for it in range(ITERS):
        last = it == ITERS - 1
        parts = split(jnp.concatenate([direction, pad_rows], axis=0))
        halo_out[it] = times(pick_ghost, parts)[: 6 * ghosts]
        halo_copies = exchange(halo_out, halo_in, halo_send, halo_recv, it, 0)
        put_vectors(dot(pick_rows, parts[0]), dot(pick_rows, parts[1]))
        if it == 0:
            for c in range(CHUNKS):
                loads[c].wait()

                def convert(i, carry, c=c):
                    here = pl.ds(pl.multiple_of(c * chunk_rows + i * 256, 256), 256)
                    high, low = split(raw[here, :])
                    tile_high[here, :] = high
                    tile_low[here, :] = low
                    return carry

                lax.fori_loop(0, chunk_rows // 256, convert, 0)
        tile_loop(True)
        backward = take_products()
        if not last:
            sums = times(hot_cols, split(backward))
            back_out[it] = sums[blocks:]
            back_copies = exchange(back_out, back_in, back_send, back_recv, it, 1)
        wait_all(halo_copies)
        extended = split(jnp.concatenate([direction, halo_in[it], pad_slots], axis=0))
        right_high, right_low = dot(pick_cols, extended[0]), dot(pick_cols, extended[1])
        if last:
            curve = column_sum(hardness * direction * direction)
            curve = curve + 2.0 * column_sum(backward * (right_high + right_low))
            norm, curve, total_x, total_d = reduce_all(
                [column_sum(residual * residual), curve, column_sum(solutions), column_sum(direction)], it
            )
            alpha = norm / curve
            solutions = solutions + alpha * direction
            totals = total_x + alpha * total_d
            ratio = totals[:, :atoms] / totals[:, atoms:]
            solutions_ref[0] = solutions[:, :atoms]
            solutions_ref[1] = solutions[:, atoms:]
            charges_ref[...] = solutions[:, :atoms] - ratio * solutions[:, atoms:]
        else:
            put_vectors(right_high, right_low)
            tile_loop(False)
            forward = take_products()
            own = sums[:blocks] + times(hot_rows, split(forward))
            wait_all(back_copies)
            returned = split(jnp.concatenate([back_in[it], pad_ghost], axis=0))
            image = hardness * direction + own + times(hot_ghost, returned)
            norm, curve, cross, square = reduce_all(
                [
                    column_sum(residual * residual), column_sum(direction * image),
                    column_sum(residual * image), column_sum(image * image),
                ], it
            )
            alpha = norm / curve
            solutions = solutions + alpha * direction
            residual = residual - alpha * image
            beta = (norm - 2.0 * alpha * cross + alpha * alpha * square) / norm
            direction = residual + beta * direction


def body(electroneg, hardness, tiles, pair_rows, pair_cols, pair_count, ghost_ids):
    sizes = tuple(lax.axis_size(name) for name in ("gx", "gy", "gz"))
    blocks, atoms = electroneg.shape[3:]
    pairs = tiles.shape[3]
    ghosts = ghost_ids.shape[4]
    ghost_row = jnp.pad(
        ghost_ids.reshape(1, 6 * ghosts), ((0, 0), (0, atoms - 6 * ghosts)), constant_values=-1
    )
    in_plane, in_line = sizes[0] * sizes[2] - 1, sizes[1] - 1
    vmem = pl.BlockSpec(memory_space=pltpu.VMEM)
    wide = 2 * atoms
    dma = pltpu.SemaphoreType.DMA
    solutions, charges = pl.pallas_call(
        functools.partial(kernel, sizes, blocks, ghosts, pairs, atoms),
        out_shape=(
            jax.ShapeDtypeStruct((2, blocks, atoms), F32),
            jax.ShapeDtypeStruct((blocks, atoms), F32),
        ),
        in_specs=[pl.BlockSpec(memory_space=pltpu.SMEM)] + [vmem] * 5 + [pl.BlockSpec(memory_space=pl.ANY)],
        out_specs=(vmem, vmem),
        scratch_shapes=[
            pltpu.VMEM((pairs * atoms, atoms), F32),
            pltpu.VMEM((pairs * atoms, atoms), BF16),
            pltpu.VMEM((pairs * atoms, atoms), BF16),
            pltpu.VMEM((pairs * 4, atoms), F32),
            pltpu.VMEM((pairs * 4, atoms), F32),
            pltpu.VMEM((ITERS, 6 * ghosts, wide), F32),
            pltpu.VMEM((ITERS, 6 * ghosts, wide), F32),
            pltpu.VMEM((ITERS - 1, 6 * ghosts, wide), F32),
            pltpu.VMEM((ITERS - 1, 6 * ghosts, wide), F32),
            pltpu.VMEM((ITERS, 8, wide), F32),
            pltpu.VMEM((ITERS, 8, wide), F32),
            pltpu.VMEM((ITERS, in_plane, 8, wide), F32),
            pltpu.VMEM((ITERS, in_line, 8, wide), F32),
            dma((CHUNKS,)),
            dma((ITERS, 6)), dma((ITERS, 6)),
            dma((ITERS - 1, 6)), dma((ITERS - 1, 6)),
            dma((ITERS, in_plane)), dma((ITERS, in_plane)),
            dma((ITERS, in_line)), dma((ITERS, in_line)),
        ],
        compiler_params=pltpu.CompilerParams(
            collective_id=0, has_side_effects=True, vmem_limit_bytes=48 * 1024 * 1024
        ),
    )(
        pair_count.reshape(1, 1),
        electroneg.reshape(blocks, atoms),
        hardness.reshape(blocks, atoms),
        pair_rows.reshape(1, pairs),
        pair_cols.reshape(1, pairs),
        ghost_row,
        tiles.reshape(pairs * atoms, atoms),
    )
    return solutions.reshape((2, 1, 1, 1, blocks, atoms)), charges.reshape((1, 1, 1, blocks, atoms))


def solution(mesh):
    return jax.shard_map(
        body,
        mesh=mesh,
        in_specs=(
            P("gx", "gy", "gz", None, None),
            P("gx", "gy", "gz", None, None),
            P("gx", "gy", "gz", None, None, None),
            P("gx", "gy", "gz", None),
            P("gx", "gy", "gz", None),
            P("gx", "gy", "gz"),
            P("gx", "gy", "gz", None, None),
        ),
        out_specs=(P(None, "gx", "gy", "gz", None, None), P("gx", "gy", "gz", None, None)),
        check_vma=False,
    )
```

profile of v0, /device:TPU:0, one launch (start us, length us, event | category | flops | bytes accessed | tf_op | source)
XLA Modules:
  0.0 65.4 jit_solution(12621555647909616858)
XLA Ops:
  1.3 0.7 %reduce = s32[6,16]{1,0:T(8,128)S(1)} reduce(s32[1,1,1,6,16]{4,2,3,1,0:T(1,128)} %param.13, s32[]{:T(128)} %constant.11), dimensions={0,1,2}, to_apply=%param.13.reduce_sub_computation | reduce | bytes 772 | tf_op args[6]
  2.0 0.1 reshape.36
  2.1 0.0 copy-start
  2.1 0.8 %copy-done = f32[1,1,1,64,128]{4,3,2,1,0:T(8,128)S(1)} copy-done((f32[1,1,1,64,128]{4,3,2,1,0:T(8,128)S(1)}, f32[1,1,1,64,128]{4,3,2,1,0:T(8,128)}, u32[]{:S(2)}) %copy-start) | copy-done | bytes 32792
  2.8 0.0 copy-start.1
  2.8 0.8 %copy-done.1 = f32[1,1,1,64,128]{4,3,2,1,0:T(8,128)S(1)} copy-done((f32[1,1,1,64,128]{4,3,2,1,0:T(8,128)S(1)}, f32[1,1,1,64,128]{4,3,2,1,0:T(8,128)}, u32[]{:S(2)}) %copy-start.1) | copy-done | bytes 32792
  3.6 0.0 copy-start.2
  3.6 0.7 %copy-done.2 = s32[1,1,1,256]{3,2,1,0:T(1,128)S(1)} copy-done((s32[1,1,1,256]{3,2,1,0:T(1,128)S(1)}, s32[1,1,1,256]{3,2,1,0:T(1,128)}, u32[]{:S(2)}) %copy-start.2) | copy-done | bytes 1048
  4.3 0.0 copy-start.3
  4.3 0.7 %copy-done.3 = s32[1,1,1,256]{3,2,1,0:T(1,128)S(1)} copy-done((s32[1,1,1,256]{3,2,1,0:T(1,128)S(1)}, s32[1,1,1,256]{3,2,1,0:T(1,128)}, u32[]{:S(2)}) %copy-start.3) | copy-done | bytes 1048
  4.9 59.2 %shard_map.86 = (f32[2,64,128]{2,1,0:T(8,128)S(1)}, f32[64,128]{1,0:T(8,128)S(1)}) custom-call(s32[1,1]{1,0:T(1,128)} %bitcast.10.count_ref, f32[64,128]{1,0:T(8,128)S(1)} %bitcast.12, f32[64,128]{1,0:T(8,128)S(1)} %bitcast.13, s32[1,256]{1,0:T(1,128)S(1)} %bitcast.15, s32[1,256]{1,0:T(1,128)S(1)} %bitcast.16, s32[1,128]{1,0:T(1,128)S(1)} %pad.4.ghost_ref, ...), custom_call_target="tpu_custom_call" | custom-call | tf_op jit(solution)/shard_map/pallas_call | solution.py:253
  64.1 0.6 copy.13
  64.8 0.6 copy.14
  (1 shorter events, 0.0 us)
Async XLA Ops:
  2.1 0.8 %copy-start = (f32[1,1,1,64,128]{4,3,2,1,0:T(8,128)S(1)}, f32[1,1,1,64,128]{4,3,2,1,0:T(8,128)}, u32[]{:S(2)}) copy-start(f32[1,1,1,64,128]{4,3,2,1,0:T(8,128)} %param.7) | copy-start | bytes 98308
  2.8 0.8 %copy-start.1 = (f32[1,1,1,64,128]{4,3,2,1,0:T(8,128)S(1)}, f32[1,1,1,64,128]{4,3,2,1,0:T(8,128)}, u32[]{:S(2)}) copy-start(f32[1,1,1,64,128]{4,3,2,1,0:T(8,128)} %param.8) | copy-start | bytes 98308
  3.6 0.7 %copy-start.2 = (s32[1,1,1,256]{3,2,1,0:T(1,128)S(1)}, s32[1,1,1,256]{3,2,1,0:T(1,128)}, u32[]{:S(2)}) copy-start(s32[1,1,1,256]{3,2,1,0:T(1,128)} %param.10) | copy-start | bytes 3076
  4.3 0.7 %copy-start.3 = (s32[1,1,1,256]{3,2,1,0:T(1,128)S(1)}, s32[1,1,1,256]{3,2,1,0:T(1,128)}, u32[]{:S(2)}) copy-start(s32[1,1,1,256]{3,2,1,0:T(1,128)} %param.11) | copy-start | bytes 3076
where the time goes:
time: 65.7 us; the launch traced here: 65.4 us
  Pallas kernels  59.2 us (90%)
  local copies, waits for them, and re-layouts  4.2 us (6%)
  between operations  1.3 us (2%)
  other arithmetic  0.7 us (1%)
    pallas_call x1, Pallas kernels, body(): pl.pallas_call(functools.partial(kernel, sizes, blocks, ghosts, pairs, at...  59.2 us
    unnamed x10, local copies, waits for them, and re-layouts  4.11 us

commit v1 on v0

--- a/solution.py
+++ b/solution.py
@@ -1,4 +1,5 @@
 import functools
+import math
 
 import jax
 import jax.numpy as jnp
@@ -9,6 +10,8 @@
 
 ITERS = 3
 CHUNKS = 8
+UNROLL = 32
+DIRECT = 32
 F32 = jnp.float32
 BF16 = jnp.bfloat16
 
@@ -30,25 +33,20 @@
     return dot(hot, parts[0]) + dot(hot, parts[1])
 
 
-def half_sums(row):
-    atoms = row.shape[1] // 2
-    sums = [jnp.sum(row[:, s * atoms : (s + 1) * atoms], axis=1, keepdims=True) for s in (0, 1)]
-    return jnp.concatenate([jnp.broadcast_to(s, (1, atoms)) for s in sums], axis=1)
-
-
 def column_sum(values):
     return jnp.sum(values, axis=0, keepdims=True)
 
 
 def kernel(
-    sizes, blocks, ghosts, pairs, atoms,
+    sizes, spreads, blocks, ghosts, pairs, atoms,
     count_ref, electroneg_ref, hardness_ref, rows_ref, cols_ref, ghost_ref, tiles_ref,
     solutions_ref, charges_ref,
     raw, tile_high, tile_low, vectors, products, halo_out, halo_in, back_out, back_in,
-    part_a, part_b, sum_a, sum_b,
-    load_sem, halo_send, halo_recv, back_send, back_recv, a_send, a_recv, b_send, b_recv,
+    load_sem, halo_send, halo_recv, back_send, back_recv, *reduce_refs,
 ):
     nx, ny, nz = sizes
+    stages = len(spreads)
+    reducers = [reduce_refs[k * stages : (k + 1) * stages] for k in range(4)]
     ix, iy, iz = lax.axis_index("gx"), lax.axis_index("gy"), lax.axis_index("gz")
     chunk_rows = pairs * atoms // CHUNKS
     loads = []
@@ -58,11 +56,13 @@
         load.start()
         loads.append(load)
 
-    plane = [
-        (lax.rem(ix + ox, nx), iy, lax.rem(iz + oz, nz))
-        for ox in range(nx) for oz in range(nz) if ox or oz
-    ]
-    line = [(ix, lax.rem(iy + oy, ny), iz) for oy in range(1, ny)]
+    def group_of(spread):
+        offsets = [(ox, oy, oz) for ox in range(spread[0]) for oy in range(spread[1]) for oz in range(spread[2])]
+        return [
+            (lax.rem(ix + ox, nx), lax.rem(iy + oy, ny), lax.rem(iz + oz, nz)) for ox, oy, oz in offsets[1:]
+        ]
+
+    groups = [group_of(spread) for spread in spreads]
     faces = []
     for axis in range(3):
         for step in (1, -1):
@@ -72,9 +72,8 @@
             faces.append((tuple(there), tuple(behind)))
 
     barrier = pltpu.get_barrier_semaphore()
-    for peer in plane + line:
+    for peer in sum(groups, []):
         pl.semaphore_signal(barrier, inc=1, device_id=peer, device_id_type=pl.DeviceIdType.MESH)
-    pl.semaphore_wait(barrier, len(plane) + len(line))
 
     def remote(src, dst, send, recv, peer):
         copy = pltpu.make_async_remote_copy(
@@ -105,17 +104,15 @@
         ]
 
     def reduce_all(rows, it):
-        zeros = jnp.zeros((8 - len(rows), 2 * atoms), F32)
-        part_a[it] = jnp.concatenate(rows + [zeros], axis=0)
-        wait_all(gathered_sum(part_a, sum_a, a_send, a_recv, it, plane))
-        total = part_a[it]
-        for k in range(len(plane)):
-            total = total + sum_a[it, k]
-        part_b[it] = total
-        wait_all(gathered_sum(part_b, sum_b, b_send, b_recv, it, line))
-        for k in range(len(line)):
-            total = total + sum_b[it, k]
-        return [half_sums(total[i : i + 1]) for i in range(len(rows))]
+        total = jnp.concatenate([row[:, :atoms] for row in rows] + [row[:, atoms:] for row in rows], axis=0)
+        for group, part, arrived, send, recv in zip(groups, *reducers):
+            part[it] = total
+            wait_all(gathered_sum(part, arrived, send, recv, it, group))
+            for k in range(len(group)):
+                total = total + arrived[it, k]
+        sums = jnp.broadcast_to(jnp.sum(total, axis=1, keepdims=True), total.shape)
+        n = len(rows)
+        return [jnp.concatenate([sums[i : i + 1], sums[n + i : n + i + 1]], axis=1) for i in range(n)]
 
     slots = 2 * atoms
     live = lax.broadcasted_iota(jnp.int32, (slots, pairs), 1) < count_ref[0, 0]
@@ -148,7 +145,7 @@
         first = [products[pl.ds(k, pairs, stride=4), :] for k in range(4)]
         return jnp.concatenate([first[0] + first[2], first[1] + first[3]], axis=1)
 
-    def tile_loop(backward):
+    def tile_loop(backward, start, stop):
         def step(i, carry):
             at = pl.ds(pl.multiple_of(i * 8, 8), 8)
             here = pl.ds(pl.multiple_of(i * 2 * atoms, 2 * atoms), 2 * atoms)
@@ -168,7 +165,9 @@
             products[at, :] = jnp.where(first_pair, out[:, :atoms], out[:, atoms:])
             return carry
 
-        lax.fori_loop(0, pairs // 2, step, 0, unroll=8)
+        lax.fori_loop(start, stop, step, 0, unroll=min(UNROLL, stop - start))
+
+    pl.semaphore_wait(barrier, sum(len(group) for group in groups))
 
     hardness = hardness_ref[...]
     hardness = jnp.concatenate([hardness, hardness], axis=1)
@@ -195,7 +194,9 @@
                     return carry
 
                 lax.fori_loop(0, chunk_rows // 256, convert, 0)
-        tile_loop(True)
+                tile_loop(True, c * pairs // (2 * CHUNKS), (c + 1) * pairs // (2 * CHUNKS))
+        else:
+            tile_loop(True, 0, pairs // 2)
         backward = take_products()
         if not last:
             sums = times(hot_cols, split(backward))
@@ -219,7 +220,7 @@
             charges_ref[...] = solutions[:, :atoms] - ratio * solutions[:, atoms:]
         else:
             put_vectors(right_high, right_low)
-            tile_loop(False)
+            tile_loop(False, 0, pairs // 2)
             forward = take_products()
             own = sums[:blocks] + times(hot_rows, split(forward))
             wait_all(back_copies)
@@ -246,12 +247,13 @@
     ghost_row = jnp.pad(
         ghost_ids.reshape(1, 6 * ghosts), ((0, 0), (0, atoms - 6 * ghosts)), constant_values=-1
     )
-    in_plane, in_line = sizes[0] * sizes[2] - 1, sizes[1] - 1
+    spreads = [sizes] if math.prod(sizes) <= DIRECT else [(sizes[0], 1, sizes[2]), (1, sizes[1], 1)]
+    peers = [math.prod(spread) - 1 for spread in spreads]
     vmem = pl.BlockSpec(memory_space=pltpu.VMEM)
     wide = 2 * atoms
     dma = pltpu.SemaphoreType.DMA
     solutions, charges = pl.pallas_call(
-        functools.partial(kernel, sizes, blocks, ghosts, pairs, atoms),
+        functools.partial(kernel, sizes, spreads, blocks, ghosts, pairs, atoms),
         out_shape=(
             jax.ShapeDtypeStruct((2, blocks, atoms), F32),
             jax.ShapeDtypeStruct((blocks, atoms), F32),
@@ -268,15 +270,13 @@
             pltpu.VMEM((ITERS, 6 * ghosts, wide), F32),
             pltpu.VMEM((ITERS - 1, 6 * ghosts, wide), F32),
             pltpu.VMEM((ITERS - 1, 6 * ghosts, wide), F32),
-            pltpu.VMEM((ITERS, 8, wide), F32),
-            pltpu.VMEM((ITERS, 8, wide), F32),
-            pltpu.VMEM((ITERS, in_plane, 8, wide), F32),
-            pltpu.VMEM((ITERS, in_line, 8, wide), F32),
             dma((CHUNKS,)),
             dma((ITERS, 6)), dma((ITERS, 6)),
             dma((ITERS - 1, 6)), dma((ITERS - 1, 6)),
-            dma((ITERS, in_plane)), dma((ITERS, in_plane)),
-            dma((ITERS, in_line)), dma((ITERS, in_line)),
+            *[pltpu.VMEM((ITERS, 8, atoms), F32) for _ in peers],
+            *[pltpu.VMEM((ITERS, n, 8, atoms), F32) for n in peers],
+            *[dma((ITERS, n)) for n in peers],
+            *[dma((ITERS, n)) for n in peers],
         ],
         compiler_params=pltpu.CompilerParams(
             collective_id=0, has_side_effects=True, vmem_limit_bytes=48 * 1024 * 1024

time: 65.7 us -> 56.4 us (0.86)
  Pallas kernels: 59.2 us -> 49.9 us
    pallas_call x1, Pallas kernels: 59.2 us -> 49.9 us  [body(): pl.pallas_call(functools.partial(kernel, sizes, spreads, blocks, ghosts,...]
where the time goes in v1:
time: 56.4 us; the launch traced here: 56.1 us
  Pallas kernels  49.9 us (88%)
  local copies, waits for them, and re-layouts  4.2 us (7%)
  between operations  1.3 us (2%)
  other arithmetic  0.7 us (1%)
    pallas_call x1, Pallas kernels, body(): pl.pallas_call(functools.partial(kernel, sizes, spreads, blocks, ghosts,...  49.9 us
    unnamed x10, local copies, waits for them, and re-layouts  4.11 us

profile of v1, /device:TPU:0, one launch (start us, length us, event | category | flops | bytes accessed | tf_op | source)
XLA Modules:
  0.0 56.1 jit_solution(18213072587847440868)
XLA Ops:
  1.3 0.7 %reduce = s32[6,16]{1,0:T(8,128)S(1)} reduce(s32[1,1,1,6,16]{4,2,3,1,0:T(1,128)} %param.13, s32[]{:T(128)} %constant.11), dimensions={0,1,2}, to_apply=%param.13.reduce_sub_computation | reduce | bytes 772 | tf_op args[6]
  2.0 0.1 reshape.36
  2.1 0.0 copy-start
  2.1 0.8 %copy-done = f32[1,1,1,64,128]{4,3,2,1,0:T(8,128)S(1)} copy-done((f32[1,1,1,64,128]{4,3,2,1,0:T(8,128)S(1)}, f32[1,1,1,64,128]{4,3,2,1,0:T(8,128)}, u32[]{:S(2)}) %copy-start) | copy-done | bytes 32792
  2.8 0.0 copy-start.1
  2.8 0.8 %copy-done.1 = f32[1,1,1,64,128]{4,3,2,1,0:T(8,128)S(1)} copy-done((f32[1,1,1,64,128]{4,3,2,1,0:T(8,128)S(1)}, f32[1,1,1,64,128]{4,3,2,1,0:T(8,128)}, u32[]{:S(2)}) %copy-start.1) | copy-done | bytes 32792
  3.6 0.0 copy-start.2
  3.6 0.7 %copy-done.2 = s32[1,1,1,256]{3,2,1,0:T(1,128)S(1)} copy-done((s32[1,1,1,256]{3,2,1,0:T(1,128)S(1)}, s32[1,1,1,256]{3,2,1,0:T(1,128)}, u32[]{:S(2)}) %copy-start.2) | copy-done | bytes 1048
  4.3 0.0 copy-start.3
  4.3 0.7 %copy-done.3 = s32[1,1,1,256]{3,2,1,0:T(1,128)S(1)} copy-done((s32[1,1,1,256]{3,2,1,0:T(1,128)S(1)}, s32[1,1,1,256]{3,2,1,0:T(1,128)}, u32[]{:S(2)}) %copy-start.3) | copy-done | bytes 1048
  4.9 49.9 %shard_map.86 = (f32[2,64,128]{2,1,0:T(8,128)S(1)}, f32[64,128]{1,0:T(8,128)S(1)}) custom-call(s32[1,1]{1,0:T(1,128)} %bitcast.10.count_ref, f32[64,128]{1,0:T(8,128)S(1)} %bitcast.12, f32[64,128]{1,0:T(8,128)S(1)} %bitcast.13, s32[1,256]{1,0:T(1,128)S(1)} %bitcast.15, s32[1,256]{1,0:T(1,128)S(1)} %bitcast.16, s32[1,128]{1,0:T(1,128)S(1)} %pad.4.ghost_ref, ...), custom_call_target="tpu_custom_call" | custom-call | tf_op jit(solution)/shard_map/pallas_call | solution.py:255
  54.9 0.6 %copy.13 = f32[2,1,1,1,64,128]{5,4,3,2,1,0:T(8,128)} copy(f32[2,1,1,1,64,128]{5,4,3,2,1,0:T(8,128)S(1)} %bitcast.11) | data formatting | bytes 131072
  55.5 0.6 %copy.14 = f32[1,1,1,64,128]{4,3,2,1,0:T(8,128)} copy(f32[1,1,1,64,128]{4,3,2,1,0:T(8,128)S(1)} %bitcast.14) | data formatting | bytes 65536
  (1 shorter events, 0.0 us)
Async XLA Ops:
  2.1 0.8 %copy-start = (f32[1,1,1,64,128]{4,3,2,1,0:T(8,128)S(1)}, f32[1,1,1,64,128]{4,3,2,1,0:T(8,128)}, u32[]{:S(2)}) copy-start(f32[1,1,1,64,128]{4,3,2,1,0:T(8,128)} %param.7) | copy-start | bytes 98308
  2.8 0.8 %copy-start.1 = (f32[1,1,1,64,128]{4,3,2,1,0:T(8,128)S(1)}, f32[1,1,1,64,128]{4,3,2,1,0:T(8,128)}, u32[]{:S(2)}) copy-start(f32[1,1,1,64,128]{4,3,2,1,0:T(8,128)} %param.8) | copy-start | bytes 98308
  3.6 0.7 %copy-start.2 = (s32[1,1,1,256]{3,2,1,0:T(1,128)S(1)}, s32[1,1,1,256]{3,2,1,0:T(1,128)}, u32[]{:S(2)}) copy-start(s32[1,1,1,256]{3,2,1,0:T(1,128)} %param.10) | copy-start | bytes 3076
  4.3 0.7 %copy-start.3 = (s32[1,1,1,256]{3,2,1,0:T(1,128)S(1)}, s32[1,1,1,256]{3,2,1,0:T(1,128)}, u32[]{:S(2)}) copy-start(s32[1,1,1,256]{3,2,1,0:T(1,128)} %param.11) | copy-start | bytes 3076

commit v2 on v1

--- a/solution.py
+++ b/solution.py
@@ -10,7 +10,7 @@
 
 ITERS = 3
 CHUNKS = 8
-UNROLL = 32
+UNROLL = 64
 DIRECT = 32
 F32 = jnp.float32
 BF16 = jnp.bfloat16
@@ -93,9 +93,12 @@
             ))
         return copies
 
+    departures = []
+
     def wait_all(copies):
+        departures.extend(copies)
         for copy in copies:
-            copy.wait()
+            copy.wait_recv()
 
     def gathered_sum(part, arrived, send, recv, it, peers):
         return [
@@ -107,7 +110,10 @@
         total = jnp.concatenate([row[:, :atoms] for row in rows] + [row[:, atoms:] for row in rows], axis=0)
         for group, part, arrived, send, recv in zip(groups, *reducers):
             part[it] = total
-            wait_all(gathered_sum(part, arrived, send, recv, it, group))
+            copies = gathered_sum(part, arrived, send, recv, it, group)
+            departures.extend(copies)
+            for copy in copies:
+                copy.wait_recv()
             for k in range(len(group)):
                 total = total + arrived[it, k]
         sums = jnp.broadcast_to(jnp.sum(total, axis=1, keepdims=True), total.shape)
@@ -161,7 +167,7 @@
                 ]
                 out = dot(lhs, jnp.concatenate(pair, axis=1))
             else:
-                out = dot_nt(all_parts, high) + dot_nt(high_part, low)
+                out = dot_nt(jnp.concatenate([all_parts, high_part], axis=1), jnp.concatenate([high, low], axis=1))
             products[at, :] = jnp.where(first_pair, out[:, :atoms], out[:, atoms:])
             return carry
 
@@ -218,6 +224,8 @@
             solutions_ref[0] = solutions[:, :atoms]
             solutions_ref[1] = solutions[:, atoms:]
             charges_ref[...] = solutions[:, :atoms] - ratio * solutions[:, atoms:]
+            for copy in departures:
+                copy.wait_send()
         else:
             put_vectors(right_high, right_low)
             tile_loop(False, 0, pairs // 2)

time: 56.4 us -> 56.1 us (level)
  no operation moved by 1% of the time
where the time goes in v2:
time: 56.1 us; the launch traced here: 55.8 us
  Pallas kernels  49.6 us (88%)
  local copies, waits for them, and re-layouts  4.2 us (7%)
  between operations  1.3 us (2%)
  other arithmetic  0.7 us (1%)
    pallas_call x1, Pallas kernels, body(): pl.pallas_call(functools.partial(kernel, sizes, spreads, blocks, ghosts,...  49.6 us
    unnamed x10, local copies, waits for them, and re-layouts  4.11 us

profile of v2, /device:TPU:0, one launch (start us, length us, event | category | flops | bytes accessed | tf_op | source)
XLA Modules:
  0.0 55.8 jit_solution(10174767642084612459)
XLA Ops:
  1.3 0.7 %reduce = s32[6,16]{1,0:T(8,128)S(1)} reduce(s32[1,1,1,6,16]{4,2,3,1,0:T(1,128)} %param.13, s32[]{:T(128)} %constant.11), dimensions={0,1,2}, to_apply=%param.13.reduce_sub_computation | reduce | bytes 772 | tf_op args[6]
  2.0 0.1 reshape.36
  2.1 0.0 copy-start
  2.1 0.8 %copy-done = f32[1,1,1,64,128]{4,3,2,1,0:T(8,128)S(1)} copy-done((f32[1,1,1,64,128]{4,3,2,1,0:T(8,128)S(1)}, f32[1,1,1,64,128]{4,3,2,1,0:T(8,128)}, u32[]{:S(2)}) %copy-start) | copy-done | bytes 32792
  2.8 0.0 copy-start.1
  2.8 0.8 %copy-done.1 = f32[1,1,1,64,128]{4,3,2,1,0:T(8,128)S(1)} copy-done((f32[1,1,1,64,128]{4,3,2,1,0:T(8,128)S(1)}, f32[1,1,1,64,128]{4,3,2,1,0:T(8,128)}, u32[]{:S(2)}) %copy-start.1) | copy-done | bytes 32792
  3.6 0.0 copy-start.2
  3.6 0.7 %copy-done.2 = s32[1,1,1,256]{3,2,1,0:T(1,128)S(1)} copy-done((s32[1,1,1,256]{3,2,1,0:T(1,128)S(1)}, s32[1,1,1,256]{3,2,1,0:T(1,128)}, u32[]{:S(2)}) %copy-start.2) | copy-done | bytes 1048
  4.3 0.0 copy-start.3
  4.3 0.7 %copy-done.3 = s32[1,1,1,256]{3,2,1,0:T(1,128)S(1)} copy-done((s32[1,1,1,256]{3,2,1,0:T(1,128)S(1)}, s32[1,1,1,256]{3,2,1,0:T(1,128)}, u32[]{:S(2)}) %copy-start.3) | copy-done | bytes 1048
  4.9 49.6 %shard_map.86 = (f32[2,64,128]{2,1,0:T(8,128)S(1)}, f32[64,128]{1,0:T(8,128)S(1)}) custom-call(s32[1,1]{1,0:T(1,128)} %bitcast.10.count_ref, f32[64,128]{1,0:T(8,128)S(1)} %bitcast.12, f32[64,128]{1,0:T(8,128)S(1)} %bitcast.13, s32[1,256]{1,0:T(1,128)S(1)} %bitcast.15, s32[1,256]{1,0:T(1,128)S(1)} %bitcast.16, s32[1,128]{1,0:T(1,128)S(1)} %pad.4.ghost_ref, ...), custom_call_target="tpu_custom_call" | custom-call | tf_op jit(solution)/shard_map/pallas_call | solution.py:263
  54.5 0.6 %copy.13 = f32[2,1,1,1,64,128]{5,4,3,2,1,0:T(8,128)} copy(f32[2,1,1,1,64,128]{5,4,3,2,1,0:T(8,128)S(1)} %bitcast.11) | data formatting | bytes 131072
  55.1 0.6 %copy.14 = f32[1,1,1,64,128]{4,3,2,1,0:T(8,128)} copy(f32[1,1,1,64,128]{4,3,2,1,0:T(8,128)S(1)} %bitcast.14) | data formatting | bytes 65536
  (1 shorter events, 0.0 us)
Async XLA Ops:
  2.1 0.8 %copy-start = (f32[1,1,1,64,128]{4,3,2,1,0:T(8,128)S(1)}, f32[1,1,1,64,128]{4,3,2,1,0:T(8,128)}, u32[]{:S(2)}) copy-start(f32[1,1,1,64,128]{4,3,2,1,0:T(8,128)} %param.7) | copy-start | bytes 98308
  2.8 0.8 %copy-start.1 = (f32[1,1,1,64,128]{4,3,2,1,0:T(8,128)S(1)}, f32[1,1,1,64,128]{4,3,2,1,0:T(8,128)}, u32[]{:S(2)}) copy-start(f32[1,1,1,64,128]{4,3,2,1,0:T(8,128)} %param.8) | copy-start | bytes 98308
  3.6 0.7 %copy-start.2 = (s32[1,1,1,256]{3,2,1,0:T(1,128)S(1)}, s32[1,1,1,256]{3,2,1,0:T(1,128)}, u32[]{:S(2)}) copy-start(s32[1,1,1,256]{3,2,1,0:T(1,128)} %param.10) | copy-start | bytes 3076
  4.3 0.7 %copy-start.3 = (s32[1,1,1,256]{3,2,1,0:T(1,128)S(1)}, s32[1,1,1,256]{3,2,1,0:T(1,128)}, u32[]{:S(2)}) copy-start(s32[1,1,1,256]{3,2,1,0:T(1,128)} %param.11) | copy-start | bytes 3076
